TPU v7x, 32 devices: a whole 2x2x4 slice. The times are simulated.
32 devices in a mesh: batch: 8 (over z, y), head: 4 (over x, core).
Axes of the slice: x: 2, y: 2, z: 4, core: 2. Of those that a mesh axis runs over, the one named last changes fastest.
Arguments:
- inputs: bfloat16 [65536, 512], P(('batch', 'head')), may hold values from -6 to 6
- attn_gain: float32 [512], replicated, may hold values from 0.5 to 1.5
- query_weight: bfloat16 [512, 512], P(None, 'head'), may hold values from -0.25 to 0.25
- key_weight: bfloat16 [512, 512], P(None, 'head'), may hold values from -0.25 to 0.25
- value_weight: bfloat16 [512, 512], P(None, 'head'), may hold values from -0.25 to 0.25
- output_weight: bfloat16 [512, 512], P('head'), may hold values from -1 to 1
- ffn_gain: float32 [512], replicated, may hold values from 0.5 to 1.5
- controller: bfloat16 [512, 2], replicated, may hold values from -0.1875 to 0.1875
- expert_in: bfloat16 [2, 512, 2048], replicated, may hold values from -0.25 to 0.25
- expert_out: bfloat16 [2, 2048, 512], replicated, may hold values from -9 to 9
- group_ids: int32 [65536], P(('batch', 'head')), may hold values from 0 to 255, as said below
- live_mask: int32 [65536], P(('batch', 'head')), may hold values from 0 to 1, as said below
- cotangent: bfloat16 [65536, 512], P(('batch', 'head')), may hold values from -6 to 6
Outputs:
- layer_out: bfloat16 [65536, 512], P(('batch', 'head'))
- input_grad: float32 [65536, 512], P(('batch', 'head'))
- attn_gain_grad: float32 [512], replicated
- query_grad: float32 [512, 512], P(None, 'head')
- key_grad: float32 [512, 512], P(None, 'head')
- value_grad: float32 [512, 512], P(None, 'head')
- output_grad: float32 [512, 512], P('head')
- ffn_gain_grad: float32 [512], replicated
- controller_grad: float32 [512, 2], replicated
- expert_in_grad: float32 [2, 512, 2048], replicated
- expert_out_grad: float32 [2, 2048, 512], replicated
Inputs may be any that keep to these rules, and one draw needn't show every extreme that they name: `group_ids`: within each aligned block of 2048 tokens (the tokens of one device) the ids count up from 0 by steps of 0 or 1; each group holds 8 to 64 tokens except the last of a block, which may hold fewer. `live_mask`: 1 except for a tail of the last group of each block; the first token of every group is 1.
All inputs are finite; a program needn't handle non-finite values.
Results may differ from a plain program's by a relative error of at most 0.017.
Values may be sent and summed in bfloat16 or wider, within the bound.
No kernel may reach another device: no remote copies, remote signals or barrier semaphores. Data moves between devices by JAX's collectives and lax.ppermute only.
A program may use at most 192 MiB of HBM per device.

v0:
```python
import jax
import jax.numpy as jnp
from jax import lax
from jax.sharding import PartitionSpec as P

HD = 64
LENGTH = 1024


eps = 1e-06
highest = lax.Precision.HIGHEST
last_dims = (((1,), (1,)), ((), ()))
first_dims = (((0,), (0,)), ((), ()))


def rms_norm(vector, gain):
    return vector * lax.rsqrt(jnp.mean(vector * vector, axis=-1, keepdims=True) + eps) * gain


def gelu_tanh(vector):
    return jax.nn.gelu(vector, approximate=True)


def causal_scores(query, keys):
    scores = jnp.einsum("qd,kd->qk", query, keys, preferred_element_type=jnp.float32) * HD ** (-0.5)
    places = lax.iota(jnp.int32, LENGTH)
    causal = places[None, :] <= places[:, None]
    return jnp.where(causal, scores, -1e30)


def attend_forward(bundle):
    query, keys, values = bundle
    scores = causal_scores(query, keys)
    peak = jnp.max(scores, axis=-1, keepdims=True)
    expo = jnp.exp(scores - peak)
    total = jnp.sum(expo, axis=-1, keepdims=True)
    probs = (expo / total).astype(jnp.bfloat16)
    context = jnp.dot(probs, values, preferred_element_type=jnp.float32)
    return (context.astype(jnp.bfloat16), (peak + jnp.log(total))[:, 0])


def attend_backward(bundle):
    query, keys, values, context_grad, logsum = bundle
    probs = jnp.exp(causal_scores(query, keys) - logsum[:, None])
    probs_low = probs.astype(jnp.bfloat16)
    value_part = lax.dot_general(
        probs_low, context_grad, first_dims, preferred_element_type=jnp.float32
    )
    prob_grad = lax.dot_general(context_grad, values, last_dims, preferred_element_type=jnp.float32)
    central = jnp.sum(prob_grad * probs, axis=-1, keepdims=True)
    score_grad = (probs * (prob_grad - central)).astype(jnp.bfloat16)
    query_part = jnp.dot(score_grad, keys, preferred_element_type=jnp.float32) * HD ** (-0.5)
    key_part = lax.dot_general(
        score_grad, query, first_dims, preferred_element_type=jnp.float32
    ) * HD ** (-0.5)
    return (
        query_part.astype(jnp.bfloat16),
        key_part.astype(jnp.bfloat16),
        value_part.astype(jnp.bfloat16),
    )


def local(
    inputs,
    attn_gain,
    query_weight,
    key_weight,
    value_weight,
    output_weight,
    ffn_gain,
    controller,
    expert_in,
    expert_out,
    group_ids,
    live_mask,
    cotangent,
):
    tokens_here = inputs.shape[0]
    local_width = query_weight.shape[1]
    local_heads = local_width // HD
    rows_in = inputs.astype(jnp.float32)
    normed = rms_norm(rows_in, attn_gain).astype(jnp.bfloat16)
    gathered = lax.all_gather(normed, "head", axis=0, tiled=True)

    def to_heads(flat):
        return (
            flat.reshape(-1, LENGTH, local_heads, HD).transpose(0, 2, 1, 3).reshape(-1, LENGTH, HD)
        )

    def from_heads(stacked):
        return (
            stacked.reshape(-1, local_heads, LENGTH, HD)
            .transpose(0, 2, 1, 3)
            .reshape(-1, local_width)
        )

    query = to_heads(
        jnp.dot(gathered, query_weight, preferred_element_type=jnp.float32).astype(jnp.bfloat16)
    )
    keys_all = to_heads(
        jnp.dot(gathered, key_weight, preferred_element_type=jnp.float32).astype(jnp.bfloat16)
    )
    values_all = to_heads(
        jnp.dot(gathered, value_weight, preferred_element_type=jnp.float32).astype(jnp.bfloat16)
    )
    context, logsum = lax.map(attend_forward, (query, keys_all, values_all))
    context_flat = from_heads(context)
    attention = lax.psum_scatter(
        jnp.dot(context_flat, output_weight, preferred_element_type=jnp.float32),
        "head",
        scatter_dimension=0,
        tiled=True,
    )
    middle = rows_in + attention
    normed2 = rms_norm(middle, ffn_gain).astype(jnp.bfloat16)
    logits = jnp.dot(normed2, controller, preferred_element_type=jnp.float32)
    slots = tokens_here // 8
    live_float = live_mask.astype(jnp.float32)
    onehot = (group_ids[:, None] == lax.iota(jnp.int32, slots)[None, :]).astype(
        jnp.float32
    ) * live_float[:, None]

    def group_softmax(logit_rows):
        expo = jnp.exp(logit_rows) * live_float[:, None]
        totals = jnp.dot(onehot.T, expo, precision=highest)
        return expo / (jnp.dot(onehot, totals, precision=highest) + (1.0 - live_float)[:, None])

    weights, softmax_back = jax.vjp(group_softmax, logits)
    weights_low = weights.astype(jnp.bfloat16)
    assign = onehot.astype(jnp.bfloat16)[None, :, :] * weights_low.T[:, :, None]
    mixed = jnp.einsum("etg,td->egd", assign, normed2, preferred_element_type=jnp.float32).astype(
        jnp.bfloat16
    )
    before = jnp.einsum("egd,edf->egf", mixed, expert_in, preferred_element_type=jnp.float32)
    active = gelu_tanh(before).astype(jnp.bfloat16)
    result = jnp.einsum(
        "egf,efd->egd", active, expert_out, preferred_element_type=jnp.float32
    ).astype(jnp.bfloat16)
    mixture = jnp.einsum("etg,egd->td", assign, result, preferred_element_type=jnp.float32)
    layer_out = (middle + mixture).astype(jnp.bfloat16)
    result_grad = jnp.einsum(
        "etg,td->egd", assign, cotangent, preferred_element_type=jnp.float32
    ).astype(jnp.bfloat16)
    assign_grad = jnp.einsum("td,egd->etg", cotangent, result, preferred_element_type=jnp.float32)
    expert_out_grad = jnp.einsum(
        "egf,egd->efd", active, result_grad, preferred_element_type=jnp.float32
    )
    active_grad = jnp.einsum(
        "egd,efd->egf", result_grad, expert_out, preferred_element_type=jnp.float32
    )
    before_grad = jax.vjp(gelu_tanh, before)[1](active_grad)[0].astype(jnp.bfloat16)
    expert_in_grad = jnp.einsum(
        "egd,egf->edf", mixed, before_grad, preferred_element_type=jnp.float32
    )
    mixed_grad = jnp.einsum(
        "egf,edf->egd", before_grad, expert_in, preferred_element_type=jnp.float32
    ).astype(jnp.bfloat16)
    assign_grad = assign_grad + jnp.einsum(
        "td,egd->etg", normed2, mixed_grad, preferred_element_type=jnp.float32
    )
    normed2_grad = jnp.einsum("etg,egd->td", assign, mixed_grad, preferred_element_type=jnp.float32)
    weight_grad = jnp.sum(assign_grad * onehot[None, :, :], axis=-1).T
    logit_grad = softmax_back(weight_grad)[0]
    controller_grad = jnp.dot(normed2.astype(jnp.float32).T, logit_grad, precision=highest)
    normed2_grad = normed2_grad + jnp.dot(
        logit_grad, controller.astype(jnp.float32).T, precision=highest
    )
    middle_back = jax.vjp(rms_norm, middle, ffn_gain)[1]
    middle_grad, ffn_gain_grad = middle_back(normed2_grad)
    middle_grad = cotangent.astype(jnp.float32) + middle_grad
    middle_low = middle_grad.astype(jnp.bfloat16)
    portion = lax.all_gather(middle_low, "head", axis=0, tiled=True)
    product = lax.dot_general(portion, output_weight, last_dims, preferred_element_type=jnp.float32)
    context_grad = product
    output_part = lax.dot_general(
        context_flat, portion, first_dims, preferred_element_type=jnp.float32
    )
    context_grad, output_grad = (context_grad, output_part)
    context_low = to_heads(context_grad.astype(jnp.bfloat16))
    query_back, key_back, value_back = lax.map(
        attend_backward, (query, keys_all, values_all, context_low, logsum)
    )
    query_flat = from_heads(query_back)
    key_flat = from_heads(key_back)
    value_flat = from_heads(value_back)
    query_grad = lax.dot_general(
        gathered, query_flat, first_dims, preferred_element_type=jnp.float32
    )
    key_grad = lax.dot_general(gathered, key_flat, first_dims, preferred_element_type=jnp.float32)
    value_grad = lax.dot_general(
        gathered, value_flat, first_dims, preferred_element_type=jnp.float32
    )
    total = lax.dot_general(query_flat, query_weight, last_dims, preferred_element_type=jnp.float32)
    total = total + lax.dot_general(
        key_flat, key_weight, last_dims, preferred_element_type=jnp.float32
    )
    normed_grad = lax.psum_scatter(
        total
        + lax.dot_general(value_flat, value_weight, last_dims, preferred_element_type=jnp.float32),
        "head",
        scatter_dimension=0,
        tiled=True,
    )
    input_back = jax.vjp(rms_norm, rows_in, attn_gain)[1]
    rows_grad, attn_gain_grad = input_back(normed_grad)
    input_grad = middle_grad + rows_grad
    query_grad, key_grad, value_grad, output_grad = lax.psum(
        (query_grad, key_grad, value_grad, output_grad), "batch"
    )
    expert_in_grad, expert_out_grad, controller_grad, ffn_gain_grad, attn_gain_grad = lax.psum(
        (expert_in_grad, expert_out_grad, controller_grad, ffn_gain_grad, attn_gain_grad),
        ("batch", "head"),
    )
    return (
        layer_out,
        input_grad,
        attn_gain_grad,
        query_grad,
        key_grad,
        value_grad,
        output_grad,
        ffn_gain_grad,
        controller_grad,
        expert_in_grad,
        expert_out_grad,
    )


def solution(mesh):
    in_specs = (
        P(("batch", "head"), None),
        P(),
        P(None, "head"),
        P(None, "head"),
        P(None, "head"),
        P("head", None),
        P(),
        P(),
        P(),
        P(),
        P(("batch", "head")),
        P(("batch", "head")),
        P(("batch", "head"), None),
    )
    out_specs = (
        P(("batch", "head"), None),
        P(("batch", "head"), None),
        P(),
        P(None, "head"),
        P(None, "head"),
        P(None, "head"),
        P("head", None),
        P(),
        P(),
        P(),
        P(),
    )
    return jax.shard_map(local, mesh=mesh, in_specs=in_specs, out_specs=out_specs, check_vma=False)
```

profile of v0, /device:TPU:0, one launch (start us, length us, event | category | flops | bytes accessed | tf_op | source)
XLA Modules:
  0.0 1196.3 jit_solution(10714187447211086830)
XLA Ops:
  14.1 61.1 %all-gather.3.cloned.1.call-done = bf16[8192,512]{1,0:T(8,128)(2,1)} async-done(((bf16[2048,512]{1,0:T(8,128)(2,1)}), bf16[8192,512]{1,0:T(8,128)(2,1)}) %all-gather.3.cloned.1.call-update) | async-done | bytes 8388624 | tf_op jit(solution)/shard_map/all_gather | solution.py:83
  75.2 7.0 convolution_convert_fusion.1
  91.3 7.0 convolution_convert_fusion.2
  107.0 7.0 convolution_convert_fusion.3
  123.0 65.9 %while.26 = (s32[]{:T(128)}, bf16[16,1024,64]{1,2,0:T(8,128)(2,1)S(1)}, f32[16,1024]{1,0:T(8,128)S(1)}, bf16[16,1024,64]{2,1,0:T(8,128)(2,1)}, bf16[16,1024,64]{...) while((s32[]{:T(128)}, bf16[16,1024,64]{1,2,0:T(8,128)(2,1)S(1)}, ...), condition=%wide.region_4.5_spmd, body=%wide.region_1.4_spmd.sunk | while | flops 284228608 | bytes 13543521 | solution.py:106
  192.9 8.1 fusion.155
  205.1 122.2 %reduce-scatter.3.cloned.1.call-done = f32[2048,512]{1,0:T(8,128)} async-done(((f32[8192,512]{1,0:T(8,128)}), f32[2048,512]{1,0:T(8,128)}) %reduce-scatter.3.cloned.1.call-update) | async-done | bytes 4194320 | tf_op jit(solution)/shard_map/reduce_scatter | solution.py:108
  341.0 4.4 fusion.72
  363.9 58.4 %all-gather.5.cloned.1.call-done = bf16[8192,512]{1,0:T(8,128)(2,1)} async-done(((bf16[2048,512]{1,0:T(8,128)(2,1)}), bf16[8192,512]{1,0:T(8,128)(2,1)}) %all-gather.5.cloned.1.call-update) | async-done | bytes 8388624 | tf_op jit(solution)/shard_map/all_gather | solution.py:172
  422.3 7.0 convolution_convert_fusion
  443.7 185.0 %while.27 = (s32[]{:T(128)}, bf16[16,1024,64]{1,2,0:T(8,128)(2,1)}, bf16[16,1024,64]{1,2,0:T(8,128)(2,1)}, bf16[16,1024,64]{1,2,0:T(8,128)(2,1)}, bf16[16,1024,6...) while((s32[]{:T(128)}, bf16[16,1024,64]{1,2,0:T(8,128)(2,1)}, ...), condition=%wide.region_11.12_spmd, body=%wide.region_9.11_spmd.sunk | while | flops 681901056 | bytes 33449072 | solution.py:180
  639.6 8.1 fusion.158
  647.7 8.3 fusion.157
  656.1 18.9 %add_add_fusion = f32[8192,512]{1,0:T(8,128)} fusion(f32[8192,512]{1,0:T(8,128)} %fusion.157, f32[8192,512]{1,0:T(8,128)} %fusion.158, bf16[8192,128]{0,1:T(8,128)(2,1)} %bitcast.241, bf16[512,128]{1,0:T(8,128)(2,1)S(1)} %copy-done.28), kind=kOutput, calls=%fused_computation.60 | convolution fusion | flops 1082130432 | bytes 52559872 | tf_op jit(solution)/shard_map/dot_general | solution.py:199
  675.0 6.5 fusion.164
  681.5 6.7 fusion.153
  689.7 5.4 fusion.78
  695.1 7.8 fusion.162
  712.2 89.1 %reduce-scatter.5.cloned.1.call-done = f32[2048,512]{1,0:T(8,128)} async-done(((f32[8192,512]{1,0:T(8,128)}), f32[2048,512]{1,0:T(8,128)}) %reduce-scatter.5.cloned.1.call-update) | async-done | bytes 4194320 | tf_op jit(solution)/shard_map/reduce_scatter | solution.py:197
  804.5 41.4 %all-reduce = (f32[512]{0:T(512)}, f32[512]{0:T(512)}, f32[512,2]{0,1:T(2,128)}) all-reduce(f32[512]{0:T(512)S(1)} %get-tuple-element.115, f32[512]{0:T(512)S(1)} %get-tuple-element.113, f32[512,2]{0,1:T(2,128)S(1)} %fusion.163), channel_id=1, replica_groups=mesh['batch'=8,'head'=4] {'batch','head'}, use_global_device_ids=true, to_apply=%region_15.16 | all-reduce | flops 2048 | bytes 16384 | tf_op jit(solution)/shard_map/psum | solution.py:210
  845.9 8.8 fusion.74
  854.7 233.1 %all-reduce.6.cloned.1.call-done = (f32[2,512,2048]{2,1,0:T(8,128)}, f32[2,2048,512]{2,1,0:T(8,128)}) async-done(((f32[2,512,2048]{2,1,0:T(8,128)}, f32[2,2048,512]{2,1,0:T(8,128)}), (f32[2,512,2048]{2,1,0:T(8,128)}, f32[2,2048,512]{2,1,0:T(8,128)})) %all-reduce.6.cloned.1.call-update) | async-done | bytes 16777232 | tf_op jit(solution)/shard_map/psum | solution.py:210
  1087.8 83.2 %all-reduce.8.cloned.1.call-done = (f32[512,128]{1,0:T(8,128)}, f32[512,128]{1,0:T(8,128)}, f32[512,128]{1,0:T(8,128)}, f32[128,512]{1,0:T(8,128)}) async-done(((f32[512,128]{1,0:T(8,128)}, f32[512,128]{1,0:T(8,128)}, f32[512,128]{1,0:T(8,128)}, f32[128,512]{1,0:T(8,128)}), (f32[512,128]{1,0:T(8,128)}, f32[512,128]{1,0:T(8,128)}, f32[512,128]{1,0:T(8,128)}, ...) | async-done | bytes 1048592 | tf_op jit(solution)/shard_map/psum | solution.py:207
  1177.8 8.0 copy.121
  (361 shorter events, 372.4 us)
Async XLA Ops:
  7.2 185.7 %copy-start = (bf16[128,512]{1,0:T(8,128)(2,1)S(1)}, bf16[128,512]{1,0:T(8,128)(2,1)}, u32[]{:S(2)}) copy-start(bf16[128,512]{1,0:T(8,128)(2,1)} %param.22) | copy-start | bytes 393220
  7.2 68.0 %copy-start.27 = (bf16[512,128]{1,0:T(8,128)(2,1)S(1)}, bf16[512,128]{1,0:T(8,128)(2,1)}, u32[]{:S(2)}) copy-start(bf16[512,128]{1,0:T(8,128)(2,1)} %param.21) | copy-start | bytes 393220
  7.2 68.0 %all-gather.3.cloned.1.call-start = ((), (), s32[]{:S(2)}) async-start(), calls=%async_computation.2 | async-start | bytes 10485760 | tf_op jit(solution)/shard_map/all_gather | solution.py:83
  14.0 313.2 %reduce-scatter.3.cloned.1.call-start = ((), (), s32[]{:S(2)}) async-start(), calls=%async_computation.3 | async-start | bytes 20971520 | tf_op jit(solution)/shard_map/reduce_scatter | solution.py:108
  201.0 126.3 %copy-start.3 = (bf16[2048,512]{1,0:T(8,128)(2,1)S(1)}, bf16[2048,512]{1,0:T(8,128)(2,1)}, u32[]{:S(2)}) copy-start(bf16[2048,512]{1,0:T(8,128)(2,1)} %param.17) | copy-start | bytes 6291460
  201.0 221.2 %all-gather.5.cloned.1.call-start = ((), (), s32[]{:S(2)}) async-start(), calls=%async_computation.4 | async-start | bytes 10485760 | tf_op jit(solution)/shard_map/all_gather | solution.py:172
  205.1 125.0 %copy-start.36 = (f32[512]{0:T(512)S(1)}, f32[512]{0:T(512)}, u32[]{:S(2)}) copy-start(f32[512]{0:T(512)} %param.23) | copy-start | bytes 6148
  330.1 29.4 %copy-start.2 = (f32[2048,512]{1,0:T(8,128)}, f32[2048,512]{1,0:T(8,128)S(1)}, u32[]{:S(2)}) copy-start(f32[2048,512]{1,0:T(8,128)S(1)} %get-tuple-element.157) | copy-start | bytes 12582916
  363.8 437.4 %reduce-scatter.5.cloned.1.call-start = ((), (), s32[]{:S(2)}) async-start(), calls=%async_computation.5 | async-start | bytes 20971520 | tf_op jit(solution)/shard_map/reduce_scatter | solution.py:197
  637.0 10.8 copy-start.10
  639.6 8.2 copy-start.12
  639.6 8.2 copy-start.26
  647.7 8.3 copy-start.28
  674.9 412.8 %all-reduce.6.cloned.1.call-start = ((), (), s32[]{:S(2)}) async-start(), calls=%async_computation.6 | async-start | bytes 33554432 | tf_op jit(solution)/shard_map/psum | solution.py:210
  688.2 482.7 %all-reduce.8.cloned.1.call-start = ((), (), s32[]{:S(2)}) async-start(), calls=%async_computation.7 | async-start | bytes 2097152 | tf_op jit(solution)/shard_map/psum | solution.py:207
  689.6 13.2 %slice-start = ((s8[8388608]{0:T(1024)(128)(4,1)}), s8[4194304]{0:T(1024)(128)(4,1)S(1)}, s32[]{:S(2)}) async-start(s8[8388608]{0:T(1024)(128)(4,1)} %bitcast.233), calls=%async_computation.8 | async-start | bytes 8388608
  695.1 7.8 slice-start.1
  695.1 7.8 copy-start.11
  709.1 92.2 %copy-start.4 = (bf16[2048,512]{1,0:T(8,128)(2,1)S(1)}, bf16[2048,512]{1,0:T(8,128)(2,1)}, u32[]{:S(2)}) copy-start(bf16[2048,512]{1,0:T(8,128)(2,1)} %param.17) | copy-start | bytes 6291460
  709.1 92.2 %copy-start.31 = (f32[2048]{0:T(1024)S(1)}, f32[2048]{0:T(1024)}, u32[]{:S(2)}) copy-start(f32[2048]{0:T(1024)} %copy-done.30) | copy-start | bytes 24580
  709.1 92.2 %copy-start.37 = (f32[512]{0:T(512)S(1)}, f32[512]{0:T(512)}, u32[]{:S(2)}) copy-start(f32[512]{0:T(512)} %param.18) | copy-start | bytes 6148
  712.1 92.3 %copy-start.33 = (f32[2048]{0:T(1024)S(1)}, f32[2048]{0:T(1024)}, u32[]{:S(2)}) copy-start(f32[2048]{0:T(1024)} %copy-done.32) | copy-start | bytes 24580
  1176.0 9.9 slice-start.2
  1177.8 8.0 slice-start.3
  (26 other events, 66.0 us)
Sparse Core Ops, SparseCore 0:
  14.2 60.9 all-gather.2
  201.1 126.0 reduce-scatter.2
  363.9 58.2 all-gather.4
  675.1 126.0 reduce-scatter.4
  808.0 279.7 all-reduce.5
  1092.1 78.8 all-reduce.7
where the time goes:
time: 1200 us
  waiting for transfers between devices  647 us (54%)
  matrix products  356 us (30%)
  local copies, waits for them, and re-layouts  83.4 us (7%)
  other arithmetic  51.8 us (4%)
  blocking collectives  41.4 us (3%)
  between operations  14.9 us (1%)
    psum x1, waiting for transfers between devices, local(): lax.psum((expert_in_grad, expert_out_grad, controller_grad, ffn_gain_grad...  233 us
    reduce_scatter x1, waiting for transfers between devices, local(): lax.psum_scatter(jnp.dot(context_flat, output_weight, preferred_element_t...  122 us
    reduce_scatter x1, waiting for transfers between devices, local(): lax.psum_scatter(total + lax.dot_general(value_flat, value_weight, last_d...  89.1 us
    psum x1, waiting for transfers between devices, local(): lax.psum((query_grad, key_grad, value_grad, output_grad), 'batch')  83.2 us
    all_gather x1, waiting for transfers between devices, local(): gathered = lax.all_gather(normed, 'head', axis=0, tiled=True)  61.1 us
    all_gather x1, waiting for transfers between devices, local(): portion = lax.all_gather(middle_low, 'head', axis=0, tiled=True)  58.4 us
    dot_general x32, matrix products, causal_scores(): jnp.einsum('qd,kd->qk', query, keys, preferred_element_type=jnp.float32)  57.4 us
    psum x1, blocking collectives, local(): lax.psum((expert_in_grad, expert_out_grad, controller_grad, ffn_gain_grad...  41.4 us
  transfers between devices with their start and end apart: 6, of which 6 were waited for; matrix products, arithmetic and copies ran while one was open for 4% of the time, Pallas kernels for 0%

commit v1 on v0

v1 whole, which is shorter than its diff:
```python
import functools

import jax
import jax.numpy as jnp
from jax import lax
from jax.experimental import pallas as pl
from jax.experimental.pallas import tpu as pltpu
from jax.sharding import PartitionSpec as P

HD = 64
LENGTH = 1024
WIDTH = 128
BF = jnp.bfloat16
F32 = jnp.float32
LOG2E = 1.4426950408889634
LN2 = 0.6931471805599453
VMEM = 56 * 2**20

eps = 1e-06
highest = lax.Precision.HIGHEST
last_dims = (((1,), (1,)), ((), ()))
first_dims = (((0,), (0,)), ((), ()))


def dot(left, right):
    return jnp.dot(left, right, preferred_element_type=F32)


def dot_last(left, right):
    return lax.dot_general(left, right, last_dims, preferred_element_type=F32)


def dot_first(left, right):
    return lax.dot_general(left, right, first_dims, preferred_element_type=F32)


def split3(value):
    high = value.astype(BF)
    rest = value - high.astype(F32)
    mid = rest.astype(BF)
    low = (rest - mid.astype(F32)).astype(BF)
    return high, mid, low


def call(body, name, grid, in_specs, out_specs, out_shape, flops, moved, exps=0, **extra):
    return pl.pallas_call(
        body,
        grid=grid,
        in_specs=in_specs,
        out_specs=out_specs,
        out_shape=out_shape,
        compiler_params=pltpu.CompilerParams(vmem_limit_bytes=VMEM),
        cost_estimate=pl.CostEstimate(
            flops=int(flops), bytes_accessed=int(moved), transcendentals=int(exps)
        ),
        name=name,
        **extra,
    )


def row_block(columns):
    return pl.BlockSpec((LENGTH, columns), lambda s: (s, 0))


def whole(*shape):
    return pl.BlockSpec(shape, lambda s: (0,) * len(shape))


def head_lanes(rows, head):
    lane = lax.broadcasted_iota(jnp.int32, (rows, WIDTH), 1)
    mine = (lane < HD) if head == 0 else (lane >= HD)
    return lane, mine, HD if head == 0 else 0


def with_extra(mine, lane, other, values, extra):
    high, mid, low = split3(extra)
    filler = jnp.zeros_like(values)
    for place, part in ((2, low), (1, mid), (0, high)):
        filler = jnp.where(lane == other + place, part, filler)
    return jnp.where(mine, values, filler)


def attend_slot(normed, weight, slot, qa_ref, k_ref, v_ref, ctx_ref):
    block = 256
    qkv = dot(normed, weight)
    q = (qkv[:, :WIDTH] * (HD**-0.5 * LOG2E)).astype(BF)
    k = qkv[:, WIDTH : 2 * WIDTH].astype(BF)
    v = qkv[:, 2 * WIDTH :].astype(BF)
    k_ref[slot] = k
    v_ref[slot] = v
    for head in range(2):
        lane, mine, other = head_lanes(LENGTH, head)
        qh = jnp.where(mine, q, jnp.zeros_like(q))
        vh = jnp.where(mine, v, (lane == other).astype(F32).astype(BF))
        q_long = qh.astype(F32)
        k_long = jnp.where(mine, k, jnp.zeros_like(k)).astype(F32)
        bound = jnp.max(jnp.sum(q_long * q_long, axis=1, keepdims=True)) * jnp.max(
            jnp.sum(k_long * k_long, axis=1, keepdims=True)
        )

        def rows_of(small):
            lane_b, mine_b, _ = head_lanes(block, head)
            for start in range(0, LENGTH, block):
                here = slice(start, start + block)
                queries = qh[here]
                scores = []
                for at in range(0, start + block, block):
                    part = dot_last(queries, k[at : at + block])
                    if at == start:
                        r = lax.broadcasted_iota(jnp.int32, (block, block), 0)
                        c = lax.broadcasted_iota(jnp.int32, (block, block), 1)
                        part = jnp.where(c <= r, part, -1e30)
                    scores.append(part)
                if not small:
                    peak = functools.reduce(
                        jnp.maximum, [jnp.max(part, axis=1, keepdims=True) for part in scores]
                    )
                    scores = [part - peak for part in scores]
                out = 0.0
                for index, part in enumerate(scores):
                    out = out + dot(
                        jnp.exp2(part).astype(BF), vh[index * block : (index + 1) * block]
                    )
                total = out[:, other : other + 1]
                logsum = jnp.log2(total)
                if not small:
                    logsum = logsum + peak
                context = (out * (1.0 / total)).astype(BF)
                qa_ref[slot, head, here] = with_extra(mine_b, lane_b, other, queries, logsum)
                if head == 1:
                    context = jnp.where(mine_b, context, ctx_ref[slot, here])
                ctx_ref[slot, here] = context

        small = bound < 1e4

        @pl.when(small)
        def _():
            rows_of(True)

        @pl.when(jnp.logical_not(small))
        def _():
            rows_of(False)


def norm_rows(rows):
    return rows * lax.rsqrt(jnp.mean(rows * rows, axis=-1, keepdims=True) + eps)


def forward_first(x_ref, gain_ref, *refs):
    slots = len(refs) - 5
    normed_ref, qa_ref, k_ref, v_ref, ctx_ref = refs[slots:]
    normed = (norm_rows(x_ref[...].astype(F32)) * gain_ref[...]).astype(BF)
    normed_ref[...] = normed
    for slot in range(slots):
        attend_slot(normed, refs[slot][...], slot, qa_ref, k_ref, v_ref, ctx_ref)


def forward_last(normed_ref, x_ref, ctx_in_ref, wo_ref, *refs):
    slots = len(refs) - 5
    qa_ref, k_ref, v_ref, ctx_ref, middle_ref = refs[slots:]
    normed = normed_ref[...]
    for slot in range(slots):
        attend_slot(normed, refs[slot][...], slot, qa_ref, k_ref, v_ref, ctx_ref)
    before = ctx_in_ref.shape[0]
    context = jnp.concatenate(
        [ctx_in_ref[i] for i in range(before)] + [ctx_ref[i] for i in range(slots)], axis=1
    )
    middle_ref[...] = x_ref[...].astype(F32) + dot(context, wo_ref[...])


def slot_outputs(slots, tokens):
    per = pl.BlockSpec((slots, LENGTH, WIDTH), lambda s: (0, s, 0))
    specs = [pl.BlockSpec((slots, 2, LENGTH, WIDTH), lambda s: (0, 0, s, 0)), per, per, per]
    flat = jax.ShapeDtypeStruct((slots, tokens, WIDTH), BF)
    shapes = [jax.ShapeDtypeStruct((slots, 2, tokens, WIDTH), BF), flat, flat, flat]
    return specs, shapes


def run_forward_first(x, gain, weights):
    tokens, width = x.shape
    specs, shapes = slot_outputs(len(weights), tokens)
    return call(
        forward_first,
        "attention_forward_first",
        (tokens // LENGTH,),
        [row_block(width), whole(1, width)] + [whole(width, 3 * WIDTH)] * len(weights),
        [row_block(width)] + specs,
        [jax.ShapeDtypeStruct((tokens, width), BF)] + shapes,
        1.5e10,
        1e7,
        1e7,
    )(x, gain, *weights)


def run_forward_last(normed, x, ctx, wo, weights):
    tokens, width = x.shape
    specs, shapes = slot_outputs(len(weights), tokens)
    ctx_spec = pl.BlockSpec((ctx.shape[0], LENGTH, WIDTH), lambda s: (0, s, 0))
    return call(
        forward_last,
        "attention_forward_last",
        (tokens // LENGTH,),
        [row_block(width), row_block(width), ctx_spec, whole(*wo.shape)]
        + [whole(width, 3 * WIDTH)] * len(weights),
        specs + [row_block(width)],
        shapes + [jax.ShapeDtypeStruct((tokens, width), F32)],
        1.5e10,
        1e7,
        1e7,
    )(normed, x, ctx, wo, *weights)


def backward_slot(
    qa_ref, k_ref, v_ref, ctx_ref, ml_ref, wo_ref, normed_ref, dqkv_ref, dw_ref, dwo_ref
):
    block = 512
    ml = ml_ref[...]
    ctx = ctx_ref[0]
    d_out = dot_last(ml, wo_ref[...]).astype(BF)
    product = d_out.astype(F32) * ctx.astype(F32)
    k = k_ref[0]
    v = v_ref[0]
    k_flip = k.T
    dks, dvs, dqs = [], [], []
    for head in range(2):
        lane, mine, other = head_lanes(LENGTH, head)
        minus = jnp.where((lane >= other) & (lane < other + 3), -1.0, 0.0).astype(BF)
        central = jnp.sum(jnp.where(mine, product, 0.0), axis=1, keepdims=True)
        d_all = with_extra(mine, lane, other, d_out, central)
        k_all = jnp.where(mine, k, minus)
        v_all = jnp.where(mine, v, minus)
        q_all = qa_ref[0, head]
        dq = [0.0] * (LENGTH // block)
        dk, dv = [], []
        for at in range(0, LENGTH, block):
            keys = k_all[at : at + block]
            values = v_all[at : at + block]
            flipped = k_flip[head * HD : (head + 1) * HD, at : at + block]
            dk_here = 0.0
            dv_here = 0.0
            for start in range(at, LENGTH, block):
                queries = q_all[start : start + block]
                d_rows = d_all[start : start + block]
                probs = jnp.exp2(dot_last(keys, queries))
                if start == at:
                    r = lax.broadcasted_iota(jnp.int32, (block, block), 0)
                    c = lax.broadcasted_iota(jnp.int32, (block, block), 1)
                    probs = jnp.where(r <= c, probs, 0.0)
                d_scores = (probs * dot_last(values, d_rows)).astype(BF)
                dv_here = dv_here + dot(probs.astype(BF), d_rows)
                dk_here = dk_here + dot(d_scores, queries)
                dq[start // block] = dq[start // block] + dot(flipped, d_scores)
            dk.append(dk_here)
            dv.append(dv_here)
        dks.append(jnp.concatenate(dk, axis=0))
        dvs.append(jnp.concatenate(dv, axis=0))
        dqs.append(jnp.concatenate(dq, axis=1))
    lane, mine, _ = head_lanes(LENGTH, 0)
    dk = (jnp.where(mine, dks[0], dks[1]) * LN2).astype(BF)
    dv = jnp.where(mine, dvs[0], dvs[1]).astype(BF)
    dq_flip = (jnp.concatenate(dqs, axis=0) * HD**-0.5).astype(BF)
    dqkv_ref[:, :WIDTH] = dq_flip.T
    dqkv_ref[:, WIDTH : 2 * WIDTH] = dk
    dqkv_ref[:, 2 * WIDTH :] = dv
    dw = dot(jnp.concatenate([dq_flip, dk.T, dv.T], axis=0), normed_ref[...])
    dwo = dot_first(ctx, ml)
    first = pl.program_id(0) == 0

    @pl.when(first)
    def _():
        dw_ref[...] = dw
        dwo_ref[...] = dwo

    @pl.when(jnp.logical_not(first))
    def _():
        dw_ref[...] += dw
        dwo_ref[...] += dwo


def run_backward(saved, index, ml, wo, normed):
    qa, k, v, ctx = saved
    tokens, width = ml.shape
    per = pl.BlockSpec((1, LENGTH, WIDTH), lambda s: (index, s, 0))
    return call(
        backward_slot,
        "attention_backward",
        (tokens // LENGTH,),
        [
            pl.BlockSpec((1, 2, LENGTH, WIDTH), lambda s: (index, 0, s, 0)),
            per,
            per,
            per,
            row_block(width),
            whole(WIDTH, width),
            row_block(width),
        ],
        [row_block(3 * WIDTH), whole(3 * WIDTH, width), whole(WIDTH, width)],
        [
            jax.ShapeDtypeStruct((tokens, 3 * WIDTH), BF),
            jax.ShapeDtypeStruct((3 * WIDTH, width), F32),
            jax.ShapeDtypeStruct((WIDTH, width), F32),
        ],
        1.5e10,
        1e7,
        1e7,
    )(qa, k, v, ctx, ml, wo, normed)


def rms_norm(vector, gain):
    return norm_rows(vector) * gain


def gelu_tanh(vector):
    return jax.nn.gelu(vector, approximate=True)


def build(mesh):
    n_head, n_batch = mesh.shape["head"], mesh.shape["batch"]
    head_bits = [1 << i for i in range(n_head.bit_length() - 1)]
    batch_bits = [1 << i for i in range(n_batch.bit_length() - 1)]

    def swap(value, axis, bit):
        size = mesh.shape[axis]
        return lax.ppermute(value, axis, [(i, i ^ bit) for i in range(size)])

    def bit_of(axis, bit):
        return (lax.axis_index(axis) // bit) % 2

    def halve(value, axis, bit):
        half = value.shape[0] // 2
        side = bit_of(axis, bit)
        sent = lax.dynamic_slice_in_dim(value, (1 - side) * half, half, 0)
        kept = lax.dynamic_slice_in_dim(value, side * half, half, 0)
        got = swap(sent, axis, bit)
        return (kept.astype(F32) + got.astype(F32)).astype(BF)

    def join(value, axis, bit):
        side = bit_of(axis, bit)
        got = swap(value, axis, bit)
        return jnp.where(
            side == 0,
            jnp.concatenate([value, got], axis=0),
            jnp.concatenate([got, value], axis=0),
        )

    def sum_everywhere(value, order):
        for axis, bit in order:
            value = halve(value, axis, bit)
        for axis, bit in order[::-1]:
            value = join(value, axis, bit)
        return value

    def sum_small(value, order):
        for axis, bit in order:
            value = value + swap(value, axis, bit)
        return value

    across = [("head", bit) for bit in head_bits[1:]] + [("batch", bit) for bit in batch_bits]
    everywhere = [("head", bit) for bit in head_bits] + [("batch", bit) for bit in batch_bits]

    def local(
        inputs,
        attn_gain,
        query_weight,
        key_weight,
        value_weight,
        output_weight,
        ffn_gain,
        controller,
        expert_in,
        expert_out,
        group_ids,
        live_mask,
        cotangent,
    ):
        tokens_here, width = inputs.shape
        pair = head_bits[0]
        w0 = jnp.concatenate([query_weight, key_weight, value_weight], axis=1)
        w1 = swap(w0, "head", 1)
        w2 = swap(w0, "head", 2)
        w3 = swap(w2, "head", 1)
        o0 = output_weight
        o1 = swap(o0, "head", 1)
        o2 = swap(o0, "head", 2)
        o3 = swap(o2, "head", 1)
        weights = [w0, w1, w2, w3]
        outs = [o0, o1, o2, o3]
        wo = jnp.concatenate(outs, axis=0)
        normed, *saved_a = run_forward_first(inputs, attn_gain[None], weights[:2])
        *saved_b, middle = run_forward_last(normed, inputs, saved_a[3], wo, weights[2:])

        normed2 = rms_norm(middle, ffn_gain).astype(BF)
        logits = jnp.dot(normed2, controller, preferred_element_type=F32)
        slots = tokens_here // 8
        live_float = live_mask.astype(F32)
        onehot = (group_ids[:, None] == lax.iota(jnp.int32, slots)[None, :]).astype(
            F32
        ) * live_float[:, None]

        def group_softmax(logit_rows):
            expo = jnp.exp(logit_rows) * live_float[:, None]
            totals = jnp.dot(onehot.T, expo, precision=highest)
            return expo / (
                jnp.dot(onehot, totals, precision=highest) + (1.0 - live_float)[:, None]
            )

        mixes, softmax_back = jax.vjp(group_softmax, logits)
        assign = onehot.astype(BF)[None, :, :] * mixes.astype(BF).T[:, :, None]
        mixed = jnp.einsum("etg,td->egd", assign, normed2, preferred_element_type=F32).astype(BF)
        result_grad = jnp.einsum(
            "etg,td->egd", assign, cotangent, preferred_element_type=F32
        ).astype(BF)

        mine = bit_of("head", pair)

        def trade(values):
            kept = lax.dynamic_index_in_dim(values, mine, 0, keepdims=False)
            sent = lax.dynamic_index_in_dim(values, 1 - mine, 0, keepdims=False)
            return jnp.concatenate([kept, swap(sent, "head", pair)], axis=0)

        def trade_back(values):
            kept, sent = values[:slots], values[slots:]
            got = swap(sent, "head", pair)
            return jnp.where(mine == 0, jnp.stack([kept, got]), jnp.stack([got, kept]))

        e_in = lax.dynamic_index_in_dim(expert_in, mine, 0, keepdims=False)
        e_out = lax.dynamic_index_in_dim(expert_out, mine, 0, keepdims=False)
        mixed_two = trade(mixed)
        result_grad_two = trade(result_grad)
        before = dot(mixed_two, e_in)
        active = gelu_tanh(before).astype(BF)
        result = trade_back(dot(active, e_out).astype(BF))
        expert_out_part = dot_first(active, result_grad_two).astype(BF)
        active_grad = dot_last(result_grad_two, e_out)
        before_grad = jax.vjp(gelu_tanh, before)[1](active_grad)[0].astype(BF)
        mixed_grad = trade_back(dot_last(before_grad, e_in).astype(BF))
        expert_in_part = dot_first(mixed_two, before_grad).astype(BF)

        mixture = jnp.einsum("etg,egd->td", assign, result, preferred_element_type=F32)
        layer_out = (middle + mixture).astype(BF)
        assign_grad = jnp.einsum("td,egd->etg", cotangent, result, preferred_element_type=F32)
        assign_grad = assign_grad + jnp.einsum(
            "td,egd->etg", normed2, mixed_grad, preferred_element_type=F32
        )
        normed2_grad = jnp.einsum("etg,egd->td", assign, mixed_grad, preferred_element_type=F32)
        weight_grad = jnp.sum(assign_grad * onehot[None, :, :], axis=-1).T
        logit_grad = softmax_back(weight_grad)[0]
        controller_grad = jnp.dot(normed2.astype(F32).T, logit_grad, precision=highest)
        normed2_grad = normed2_grad + jnp.dot(
            logit_grad, controller.astype(F32).T, precision=highest
        )
        middle_grad, ffn_gain_grad = jax.vjp(rms_norm, middle, ffn_gain)[1](normed2_grad)
        middle_grad = cotangent.astype(F32) + middle_grad
        middle_low = middle_grad.astype(BF)

        quarter = expert_in_part.shape[1] // 4
        payload = [
            jnp.concatenate(
                [expert_in_part[:, i * quarter : (i + 1) * quarter] for i in range(4)], axis=0
            ),
            expert_out_part,
        ]
        payload = jnp.concatenate(payload, axis=0)
        unit = payload.shape[0] // 16
        cuts = [0, 6 * unit, 11 * unit, 16 * unit]
        turned = [
            across,
            across[1:] + across[:1],
            across[2:3] + across[:2] + across[3:],
        ]
        summed = [
            sum_everywhere(payload[low:high], order)
            for low, high, order in zip(cuts[:-1], cuts[1:], turned)
        ]

        grads = [None] * 4
        flats = [None] * 4

        def backward(slot):
            saved, index = (saved_a, slot) if slot < 2 else (saved_b, slot - 2)
            flats[slot], dw, dwo = run_backward(saved, index, middle_low, outs[slot], normed)
            return jnp.concatenate([dw, dwo], axis=0)

        third = backward(3)
        third_got = swap(third.astype(BF), "head", 1)
        second = backward(2) + third_got.astype(F32)
        second_got = swap(second.astype(BF), "head", 2)
        first = backward(1)
        first_got = swap(first.astype(BF), "head", 1)
        own = backward(0) + second_got.astype(F32) + first_got.astype(F32)
        own = own.astype(BF)
        weight_sum = sum_everywhere(own, [("batch", bit) for bit in batch_bits]).astype(F32)
        query_grad = weight_sum[:WIDTH].T
        key_grad = weight_sum[WIDTH : 2 * WIDTH].T
        value_grad = weight_sum[2 * WIDTH : 3 * WIDTH].T
        output_grad = weight_sum[3 * WIDTH :]

        normed_grad = dot_last(
            jnp.concatenate(flats, axis=1), jnp.concatenate(weights, axis=1)
        )
        rows_in = inputs.astype(F32)
        rows_grad, attn_gain_grad = jax.vjp(rms_norm, rows_in, attn_gain)[1](normed_grad)
        input_grad = middle_grad + rows_grad

        small = jnp.concatenate([ffn_gain_grad[None], controller_grad.T], axis=0)
        small = sum_small(small, everywhere)
        attn_gain_grad = sum_small(attn_gain_grad[None], everywhere)[0]

        total = jnp.concatenate(summed, axis=0)
        other = swap(total, "head", pair)
        both = jnp.where(mine == 0, jnp.stack([total, other]), jnp.stack([other, total]))
        split = payload.shape[0] // 2
        expert_in_grad = (
            both[:, :split]
            .reshape(2, 4, width, quarter)
            .transpose(0, 2, 1, 3)
            .reshape(2, width, 4 * quarter)
            .astype(F32)
        )
        expert_out_grad = both[:, split:].astype(F32)
        return (
            layer_out,
            input_grad,
            attn_gain_grad,
            query_grad,
            key_grad,
            value_grad,
            output_grad,
            small[0],
            small[1:].T,
            expert_in_grad,
            expert_out_grad,
        )

    return local


def solution(mesh):
    in_specs = (
        P(("batch", "head"), None),
        P(),
        P(None, "head"),
        P(None, "head"),
        P(None, "head"),
        P("head", None),
        P(),
        P(),
        P(),
        P(),
        P(("batch", "head")),
        P(("batch", "head")),
        P(("batch", "head"), None),
    )
    out_specs = (
        P(("batch", "head"), None),
        P(("batch", "head"), None),
        P(),
        P(None, "head"),
        P(None, "head"),
        P(None, "head"),
        P("head", None),
        P(),
        P(),
        P(),
        P(),
    )
    return jax.shard_map(
        build(mesh), mesh=mesh, in_specs=in_specs, out_specs=out_specs, check_vma=False
    )
```

time: 1200 us -> 337 us (0.28)
  waiting for transfers between devices: 647 us -> 73.8 us
  matrix products: 356 us -> 38.2 us
  Pallas kernels: 0 us -> 95.2 us
  local copies, waits for them, and re-layouts: 83.4 us -> 22.4 us
  starting transfers between devices: 0.25 us -> 45.8 us
  blocking collectives: 41.4 us -> 0 us
  between operations: 14.9 us -> 2 us
    dot_general x139 -> x16, matrix products: 350 us -> 31.9 us  [the longest x3 10.7 us: dot_last(): return lax.dot_general(left, right, last_dims, preferred_element_type=F32)]
    psum x2 -> x0, waiting for transfers between devices: 316 us -> none  [the longest x1 233 us: local(): lax.psum((expert_in_grad, expert_out_grad, controller_grad, ffn_gain_grad...]
    reduce_scatter x2 -> x0, waiting for transfers between devices: 211 us -> none  [the longest x1 122 us: local(): lax.psum_scatter(jnp.dot(context_flat, output_weight, preferred_element_t...]
    all_gather x2 -> x0, waiting for transfers between devices: 119 us -> none  [the longest x1 61.1 us: local(): gathered = lax.all_gather(normed, 'head', axis=0, tiled=True)]
    pallas_call x0 -> x6, Pallas kernels: none -> 95.2 us  [the longest x4 55.9 us: run_backward(): call(backward_slot, 'attention_backward', (tokens // LENGTH,), [pl.BlockS...]
    ppermute x0 -> x54, waiting for transfers between devices: none -> 73.8 us  [swap(): return lax.ppermute(value, axis, [(i, i ^ bit) for i in range(size)])]
    ppermute x0 -> x54, starting transfers between devices: none -> 45.8 us  [swap(): return lax.ppermute(value, axis, [(i, i ^ bit) for i in range(size)])]
    psum x1 -> x0, blocking collectives: 41.4 us -> none  [local(): lax.psum((expert_in_grad, expert_out_grad, controller_grad, ffn_gain_grad...]
  transfers between devices with their start and end apart: 6 -> 54, of which waited for: 6 -> 21; matrix products, arithmetic and copies ran while one was open for 4% -> 26% of each run, Pallas kernels for 0% -> 22%
where the time goes in v1:
time: 337 us; the launch traced here: 334 us
  Pallas kernels  95.2 us (28%)
  waiting for transfers between devices  73.8 us (22%)
  other arithmetic  56.8 us (17%)
  starting transfers between devices  45.8 us (14%)
  matrix products  38.2 us (11%)
  local copies, waits for them, and re-layouts  22.4 us (7%)
    ppermute x54, waiting for transfers between devices, swap(): return lax.ppermute(value, axis, [(i, i ^ bit) for i in range(size)])  73.8 us
    pallas_call x4, Pallas kernels, run_backward(): call(backward_slot, 'attention_backward', (tokens // LENGTH,), [pl.BlockS...  55.9 us
    ppermute x54, starting transfers between devices, swap(): return lax.ppermute(value, axis, [(i, i ^ bit) for i in range(size)])  45.8 us
    pallas_call x1, Pallas kernels, run_forward_last(): call(forward_last, 'attention_forward_last', (tokens // LENGTH,), [row_bl...  20.8 us
    pallas_call x1, Pallas kernels, run_forward_first(): call(forward_first, 'attention_forward_first', (tokens // LENGTH,), [row_...  18.5 us
    unnamed x90, local copies, waits for them, and re-layouts  12 us
    dot_general x3, matrix products, dot_last(): return lax.dot_general(left, right, last_dims, preferred_element_type=F32)  10.7 us
    select_n x1, other arithmetic, local(): jnp.where(mine == 0, jnp.stack([total, other]), jnp.stack([other, total]))  7.98 us
  transfers between devices with their start and end apart: 54, of which 21 were waited for; matrix products, arithmetic and copies ran while one was open for 26% of the time, Pallas kernels for 22%

profile of v1, /device:TPU:0, one launch (start us, length us, event | category | flops | bytes accessed | tf_op | source)
XLA Modules:
  0.0 334.3 jit_solution(8600473238282763096)
XLA Ops:
  0.7 3.0 collective-permute-start.2
  20.4 18.5 %attention_forward_first.1 = (bf16[2048,512]{1,0:T(8,128)(2,1)}, bf16[2,2,2048,128]{3,2,1,0:T(8,128)(2,1)}, bf16[2,2048,128]{2,1,0:T(8,128)(2,1)}, bf16[2,2048,128]{2,1,0:T(8,128)(2,1)}, bf16[2,2048,128]{2,1,0:T(8,128)(2,1)}) custom-call(bf16[2048,512]{1,0:T(8,128)(2,1)} %x_ref.3, f32[1,512]{1,0:T(1,128)} %bitcast.107, ...), custom_call_target="tpu_custom_call" | custom-call | flops 15000000512 | bytes 10000000 | tf_op jit(solution)/shard_map/attention_forward_first/pallas_call | solution.py:182
  40.9 20.8 %attention_forward_last.1 = (bf16[2,2,2048,128]{3,2,1,0:T(8,128)(2,1)}, bf16[2,2048,128]{2,1,0:T(8,128)(2,1)}, bf16[2,2048,128]{2,1,0:T(8,128)(2,1)}, bf16[2,2048,128]{2,1,0:T(8,128)(2,1)}, f32[2048,512]{1,0:T(8,128)}) custom-call(bf16[2048,512]{1,0:T(8,128)(2,1)} %get-tuple-element.33.normed_ref, bf16[2048,512]{1,0:T(8,128)(2,1)} %x_ref.3, ...), custom_call_target="tpu_custom_call" | custom-call | flops 15000000512 | bytes 10000000 | tf_op jit(solution)/shard_map/attention_forward_last/pallas_call | solution.py:199
  78.8 3.7 %fusion.22 = bf16[512,2048]{1,0:T(8,128)(2,1)S(1)} fusion(f32[512,2048]{1,0:T(8,128)S(1)} %fusion.64, bf16[2,2048,512]{2,1,0:T(8,128)(2,1)S(1)} %copy-done.36, s32[]{:T(128)S(6)} %select_n.350, bf16[256,512]{1,0:T(8,128)(2,1)S(1)} %collective-permute-done.8, bf16[256,512]{1,0:T(8,128)(2,1)S(1)} %get-tuple-element.84), kind=kOutput, calls=%fused_computation.32 | convolution fusion | flops 1095761920 | bytes 8912900 | tf_op jit(solution)/shard_map/dot_general | solution.py:30
  109.4 13.9 %attention_backward.7 = (bf16[2048,384]{1,0:T(8,128)(2,1)}, f32[384,512]{1,0:T(8,128)}, f32[128,512]{1,0:T(8,128)}) custom-call(bf16[2,2,2048,128]{3,2,1,0:T(8,128)(2,1)} %get-tuple-element.41.qa_ref, bf16[2,2048,128]{2,1,0:T(8,128)(2,1)} %get-tuple-element.42.k_ref, bf16[2,2048,128]{2,1,0:T(8,128)(2,1)} %get-tuple-element.43.v_ref, ...), custom_call_target="tpu_custom_call" | custom-call | flops 15000000512 | bytes 10000000 | tf_op jit(solution)/shard_map/attention_backward/pallas_call | solution.py:284
  125.7 14.1 %attention_backward.4 = (bf16[2048,384]{1,0:T(8,128)(2,1)}, f32[384,512]{1,0:T(8,128)}, f32[128,512]{1,0:T(8,128)}) custom-call(bf16[2,2,2048,128]{3,2,1,0:T(8,128)(2,1)} %get-tuple-element.36.qa_ref, bf16[2,2048,128]{2,1,0:T(8,128)(2,1)} %get-tuple-element.37.k_ref, bf16[2,2048,128]{2,1,0:T(8,128)(2,1)} %get-tuple-element.38.v_ref, ...), custom_call_target="tpu_custom_call" | custom-call | flops 15000000512 | bytes 10000000 | tf_op jit(solution)/shard_map/attention_backward/pallas_call | solution.py:284
  139.8 13.9 %attention_backward.6 = (bf16[2048,384]{1,0:T(8,128)(2,1)}, f32[384,512]{1,0:T(8,128)}, f32[128,512]{1,0:T(8,128)}) custom-call(bf16[2,2,2048,128]{3,2,1,0:T(8,128)(2,1)} %get-tuple-element.41.qa_ref, bf16[2,2048,128]{2,1,0:T(8,128)(2,1)} %get-tuple-element.42.k_ref, bf16[2,2048,128]{2,1,0:T(8,128)(2,1)} %get-tuple-element.43.v_ref, ...), custom_call_target="tpu_custom_call" | custom-call | flops 15000000512 | bytes 10000000 | tf_op jit(solution)/shard_map/attention_backward/pallas_call | solution.py:284
  153.7 14.1 %attention_backward.5 = (bf16[2048,384]{1,0:T(8,128)(2,1)}, f32[384,512]{1,0:T(8,128)}, f32[128,512]{1,0:T(8,128)}) custom-call(bf16[2,2,2048,128]{3,2,1,0:T(8,128)(2,1)} %get-tuple-element.36.qa_ref, bf16[2,2048,128]{2,1,0:T(8,128)(2,1)} %get-tuple-element.37.k_ref, bf16[2,2048,128]{2,1,0:T(8,128)(2,1)} %get-tuple-element.38.v_ref, ...), custom_call_target="tpu_custom_call" | custom-call | flops 15000000512 | bytes 10000000 | tf_op jit(solution)/shard_map/attention_backward/pallas_call | solution.py:284
  186.9 6.8 %collective-permute-done.39 = bf16[160,512]{1,0:T(8,128)(2,1)S(1)} collective-permute-done((bf16[160,512]{1,0:T(8,128)(2,1)S(1)}, bf16[160,512]{1,0:T(8,128)(2,1)S(1)}, u32[]{:S(2)}, u32[]{:S(2)}) %collective-permute-start.39) | collective-permute-done | bytes 163872 | tf_op jit(solution)/shard_map/ppermute | solution.py:324
  194.3 4.8 %collective-permute-done.47 = bf16[160,512]{1,0:T(8,128)(2,1)S(1)} collective-permute-done((bf16[160,512]{1,0:T(8,128)(2,1)S(1)}, bf16[160,512]{1,0:T(8,128)(2,1)S(1)}, u32[]{:S(2)}, u32[]{:S(2)}) %collective-permute-start.47) | collective-permute-done | bytes 163872 | tf_op jit(solution)/shard_map/ppermute | solution.py:324
  206.7 3.9 %collective-permute-done.41 = bf16[80,512]{1,0:T(8,128)(2,1)S(1)} collective-permute-done((bf16[80,512]{1,0:T(8,128)(2,1)S(1)}, bf16[80,512]{1,0:T(8,128)(2,1)S(1)}, u32[]{:S(2)}, u32[]{:S(2)}) %collective-permute-start.41) | collective-permute-done | bytes 81952 | tf_op jit(solution)/shard_map/ppermute | solution.py:324
  212.6 7.9 %collective-permute-done.49 = bf16[80,512]{1,0:T(8,128)(2,1)S(1)} collective-permute-done((bf16[80,512]{1,0:T(8,128)(2,1)S(1)}, bf16[80,512]{1,0:T(8,128)(2,1)S(1)}, u32[]{:S(2)}, u32[]{:S(2)}) %collective-permute-start.49) | collective-permute-done | bytes 81952 | tf_op jit(solution)/shard_map/ppermute | solution.py:324
  220.7 3.0 collective-permute-start.32
  224.0 8.3 %collective-permute-done.32 = bf16[96,512]{1,0:T(8,128)(2,1)S(1)} collective-permute-done((bf16[96,512]{1,0:T(8,128)(2,1)S(1)}, bf16[96,512]{1,0:T(8,128)(2,1)S(1)}, u32[]{:S(2)}, u32[]{:S(2)}) %collective-permute-start.32) | collective-permute-done | bytes 98336 | tf_op jit(solution)/shard_map/ppermute | solution.py:324
  232.6 5.5 %collective-permute-done.33 = bf16[96,512]{1,0:T(8,128)(2,1)S(1)} collective-permute-done((bf16[96,512]{1,0:T(8,128)(2,1)S(1)}, bf16[96,512]{1,0:T(8,128)(2,1)S(1)}, u32[]{:S(2)}, u32[]{:S(2)}) %collective-permute-start.33) | collective-permute-done | bytes 98336 | tf_op jit(solution)/shard_map/ppermute | solution.py:324
  240.7 5.4 %collective-permute-done.34 = bf16[192,512]{1,0:T(8,128)(2,1)S(1)} collective-permute-done((bf16[192,512]{1,0:T(8,128)(2,1)S(1)}, bf16[192,512]{1,0:T(8,128)(2,1)S(1)}, u32[]{:S(2)}, u32[]{:S(2)}) %collective-permute-start.34) | collective-permute-done | bytes 196640 | tf_op jit(solution)/shard_map/ppermute | solution.py:324
  247.9 5.2 %collective-permute-done.43 = bf16[320,512]{1,0:T(8,128)(2,1)S(1)} collective-permute-done((bf16[320,512]{1,0:T(8,128)(2,1)S(1)}, bf16[320,512]{1,0:T(8,128)(2,1)S(1)}, u32[]{:S(2)}, u32[]{:S(2)}) %collective-permute-start.43) | collective-permute-done | bytes 327712 | tf_op jit(solution)/shard_map/ppermute | solution.py:324
  264.5 4.3 %collective-permute-done.36 = bf16[768,512]{1,0:T(8,128)(2,1)S(1)} collective-permute-done((bf16[768,512]{1,0:T(8,128)(2,1)S(1)}, bf16[768,512]{1,0:T(8,128)(2,1)S(1)}, u32[]{:S(2)}, u32[]{:S(2)}) %collective-permute-start.36) | collective-permute-done | bytes 786464 | tf_op jit(solution)/shard_map/ppermute | solution.py:324
  269.5 4.4 %fusion.151 = (bf16[1,4096,512]{2,1,0:T(8,128)(2,1)}, bf16[4096,512]{1,0:T(8,128)(2,1)}) fusion(bf16[1280,512]{1,0:T(8,128)(2,1)S(1)} %maximum_select_fusion.3, bf16[1280,512]{1,0:T(8,128)(2,1)S(1)} %maximum_select_fusion.2, bf16[1536,512]{1,0:T(8,128)(2,1)S(1)} %maximum_select_fusion.1), kind=kLoop, calls=%fused_computation.233 | loop fusion | flops 12582912 | bytes 12582912 | tf_op jit(solution)/shard_map/stack | solution.py:511
  276.3 5.7 %fusion.28 = (f32[512]{0:T(512)S(1)}, f32[2048]{0:T(1024)S(1)}, f32[2048,512]{1,0:T(8,128)}) fusion(bf16[2048,512]{1,0:T(8,128)(2,1)S(1)} %copy-done.8, f32[2048]{0:T(1024)S(1)} %copy-done.29, f32[512]{0:T(512)S(1)} %copy-done.35, bf16[512,1536]{1,0:T(8,128)(2,1)S(1)} %copy-done.34, bf16[2048,384]{1,0:T(8,128)(2,1)S(1)} %copy-done.37, ...), kind=kOutput, calls=%fused_computation.38 | convolution fusion | flops 3253728768 | bytes 14176256 | tf_op jit(solution)/shard_map/dot_general | solution.py:30
  295.4 7.8 %fusion.24 = f32[2048,512]{1,0:T(8,128)} fusion(bf16[2048,512]{1,0:T(8,128)(2,1)} %x_ref.3, f32[2048,512]{1,0:T(8,128)} %get-tuple-element.97, f32[2048]{0:T(1024)S(1)} %multiply_multiply_fusion.2, f32[2048]{0:T(1024)S(1)} %copy-done.29, f32[512]{0:T(512)S(1)} %copy-done.35, f32[2048,512]{1,0:T(8,128)} %get-tuple-element.35, ...), kind=kLoop, calls=%fused_computation.34 | loop fusion | flops 14680064 | bytes 21008384 | tf_op jit(solution)/shard_map/add | solution.py:503
  316.3 8.0 %maximum_select_fusion = bf16[2,4096,512]{2,1,0:T(8,128)(2,1)S(1)} fusion(bf16[1,4096,512]{2,1,0:T(8,128)(2,1)} %bitcast.27, bf16[1,4096,512]{2,1,0:T(8,128)(2,1)} %get-tuple-element.72, pred[]{:T(512)S(6)} %eq.83), kind=kLoop, calls=%fused_computation | loop fusion | flops 12582912 | bytes 16777216 | tf_op jit(solution)/shard_map/jit(_where)/select_n | solution.py:511
  324.3 4.1 %slice_convert_fusion = (f32[2,2048,512]{2,1,0:T(8,128)}, bf16[2,2048,512]{2,1,0:T(8,128)(2,1)S(1)}) fusion(bf16[2,4096,512]{2,1,0:T(8,128)(2,1)S(1)} %maximum_select_fusion), kind=kLoop, calls=%fused_computation.39 | loop fusion | flops 2097152 | bytes 20971520 | tf_op jit(solution)/shard_map/convert_element_type | solution.py:520
  329.6 4.4 %copy.33 = f32[2,4,64,8,512]{4,3,1,2,0:T(8,128)} copy(f32[2,4,64,8,512]{4,3,2,1,0:T(8,128)S(1)} %convert_bitcast_fusion) | data formatting | bytes 16777216 | tf_op jit(solution)/shard_map/convert_element_type | solution.py:518
  (296 shorter events, 140.9 us)
Async XLA Ops:
  0.7 14.9 %collective-permute-start.2 = (bf16[128,512]{1,0:T(8,128)(2,1)}, bf16[128,512]{1,0:T(8,128)(2,1)}, u32[]{:S(2)}, u32[]{:S(2)}) collective-permute-start(bf16[128,512]{1,0:T(8,128)(2,1)} %wo_ref.1), channel_id=1, source_target_pairs={{0,2},{1,3},{2,0},{3,1},{4,6},{5,7},{6,4},{7,5},{8,10},{9,11},{10,... | collective-permute-start | bytes 393224 | tf_op jit(solution)/shard_map/ppermute | solution.py:324
  3.7 13.4 %collective-permute-start.1 = (bf16[128,512]{1,0:T(8,128)(2,1)}, bf16[128,512]{1,0:T(8,128)(2,1)}, u32[]{:S(2)}, u32[]{:S(2)}) collective-permute-start(bf16[128,512]{1,0:T(8,128)(2,1)} %wo_ref.1), channel_id=1, source_target_pairs={{0,1},{1,0},{2,3},{3,2},{4,5},{5,4},{6,7},{7,6},{8,9},{9,8},{10,11... | collective-permute-start | bytes 393224 | tf_op jit(solution)/shard_map/ppermute | solution.py:324
  20.4 19.7 %collective-permute-start.5 = (bf16[512,384]{1,0:T(8,128)(2,1)S(1)}, bf16[512,384]{1,0:T(8,128)(2,1)S(1)}, u32[]{:S(2)}, u32[]{:S(2)}) collective-permute-start(bf16[512,384]{1,0:T(8,128)(2,1)S(1)} %collective-permute-done.4.refs_0_), channel_id=1, source_target_pairs={{0,1},{1,0},{2,3},{3,2},{4,5},{5,4},{6,7},{7,6},{8,9},{9,8},{10,11... | collective-permute-start | bytes 1179656 | tf_op jit(solution)/shard_map/ppermute | solution.py:324
  78.3 16.7 %collective-permute-start.7 = (bf16[256,512]{1,0:T(8,128)(2,1)S(1)}, bf16[256,512]{1,0:T(8,128)(2,1)S(1)}, u32[]{:S(2)}, u32[]{:S(2)}) collective-permute-start(bf16[256,512]{1,0:T(8,128)(2,1)S(1)} %get-tuple-element.87), channel_id=1, source_target_pairs={{0,1},{1,0},{2,3},{3,2},{4,5},{5,4},{6,7},{7,6},{8,9},{9,8},{10,11... | collective-permute-start | bytes 786440 | tf_op jit(solution)/shard_map/ppermute | solution.py:324
  89.3 80.6 %collective-permute-start.37 = (bf16[640,512]{1,0:T(8,128)(2,1)}, bf16[640,512]{1,0:T(8,128)(2,1)}, u32[]{:S(2)}, u32[]{:S(2)}) collective-permute-start(bf16[640,512]{1,0:T(8,128)(2,1)} %fusion.117), channel_id=1, source_target_pairs={{0,4},{4,0},{8,12},{12,8},{16,20},{20,16},{24,28},{28,24},{1,5},{5... | collective-permute-start | bytes 1966088 | tf_op jit(solution)/shard_map/ppermute | solution.py:324
  91.8 80.8 %collective-permute-start.45 = (bf16[640,512]{1,0:T(8,128)(2,1)}, bf16[640,512]{1,0:T(8,128)(2,1)}, u32[]{:S(2)}, u32[]{:S(2)}) collective-permute-start(bf16[640,512]{1,0:T(8,128)(2,1)} %constant_dynamic-slice_fusion.3), channel_id=1, source_target_pairs={{0,8},{4,12},{8,0},{12,4},{16,24},{20,28},{24,16},{28,20},{1,9},{5... | collective-permute-start | bytes 1966088 | tf_op jit(solution)/shard_map/ppermute | solution.py:324
  94.5 80.1 %collective-permute-start.29 = (bf16[768,512]{1,0:T(8,128)(2,1)}, bf16[768,512]{1,0:T(8,128)(2,1)}, u32[]{:S(2)}, u32[]{:S(2)}) collective-permute-start(bf16[768,512]{1,0:T(8,128)(2,1)} %constant_dynamic-slice_fusion.10), channel_id=1, source_target_pairs={{0,2},{1,3},{2,0},{3,1},{4,6},{5,7},{6,4},{7,5},{8,10},{9,11},{10,... | collective-permute-start | bytes 2359304 | tf_op jit(solution)/shard_map/ppermute | solution.py:324
  106.7 140.0 %collective-permute-start.24 = (f32[3,512]{1,0:T(4,128)S(1)}, f32[3,512]{1,0:T(4,128)S(1)}, u32[]{:S(2)}, u32[]{:S(2)}) collective-permute-start(f32[3,512]{1,0:T(4,128)S(1)} %pad_maximum_fusion.11), channel_id=1, source_target_pairs={{0,1},{1,0},{2,3},{3,2},{4,5},{5,4},{6,7},{7,6},{8,9},{9,8},{10,11... | collective-permute-start | bytes 18440 | tf_op jit(solution)/shard_map/ppermute | solution.py:324
  125.5 52.2 %collective-permute-start.15 = (bf16[512,512]{1,0:T(8,128)(2,1)S(1)}, bf16[512,512]{1,0:T(8,128)(2,1)}, u32[]{:S(2)}, u32[]{:S(2)}) collective-permute-start(bf16[512,512]{1,0:T(8,128)(2,1)S(1)} %pad_maximum_fusion.5), channel_id=1, source_target_pairs={{0,1},{1,0},{2,3},{3,2},{4,5},{5,4},{6,7},{7,6},{8,9},{9,8},{10,11... | collective-permute-start | bytes 1572872 | tf_op jit(solution)/shard_map/ppermute | solution.py:324
  170.0 50.8 %collective-permute-start.17 = (bf16[512,512]{1,0:T(8,128)(2,1)S(1)}, bf16[512,512]{1,0:T(8,128)(2,1)S(1)}, u32[]{:S(2)}, u32[]{:S(2)}) collective-permute-start(bf16[512,512]{1,0:T(8,128)(2,1)S(1)} %pad_maximum_fusion.6), channel_id=1, source_target_pairs={{0,1},{1,0},{2,3},{3,2},{4,5},{5,4},{6,7},{7,6},{8,9},{9,8},{10,11... | collective-permute-start | bytes 1572872 | tf_op jit(solution)/shard_map/ppermute | solution.py:324
  177.7 22.9 %collective-permute-start.30 = (bf16[384,512]{1,0:T(8,128)(2,1)S(1)}, bf16[384,512]{1,0:T(8,128)(2,1)S(1)}, u32[]{:S(2)}, u32[]{:S(2)}) collective-permute-start(bf16[384,512]{1,0:T(8,128)(2,1)S(1)} %constant_dynamic-slice_fusion.9), channel_id=1, source_target_pairs={{0,4},{4,0},{8,12},{12,8},{16,20},{20,16},{24,28},{28,24},{1,5},{5... | collective-permute-start | bytes 1179656 | tf_op jit(solution)/shard_map/ppermute | solution.py:324
  182.5 41.3 %collective-permute-start.16 = (bf16[512,512]{1,0:T(8,128)(2,1)S(1)}, bf16[512,512]{1,0:T(8,128)(2,1)S(1)}, u32[]{:S(2)}, u32[]{:S(2)}) collective-permute-start(bf16[512,512]{1,0:T(8,128)(2,1)S(1)} %fusion.96), channel_id=1, source_target_pairs={{0,2},{1,3},{2,0},{3,1},{4,6},{5,7},{6,4},{7,5},{8,10},{9,11},{10,... | collective-permute-start | bytes 1572872 | tf_op jit(solution)/shard_map/ppermute | solution.py:324
  203.5 17.1 %collective-permute-start.31 = (bf16[192,512]{1,0:T(8,128)(2,1)S(1)}, bf16[192,512]{1,0:T(8,128)(2,1)S(1)}, u32[]{:S(2)}, u32[]{:S(2)}) collective-permute-start(bf16[192,512]{1,0:T(8,128)(2,1)S(1)} %constant_dynamic-slice_fusion.8), channel_id=1, source_target_pairs={{0,8},{4,12},{8,0},{12,4},{16,24},{20,28},{24,16},{28,20},{1,9},{5... | collective-permute-start | bytes 589832 | tf_op jit(solution)/shard_map/ppermute | solution.py:324
  220.5 18.0 %collective-permute-start.42 = (bf16[160,512]{1,0:T(8,128)(2,1)S(1)}, bf16[160,512]{1,0:T(8,128)(2,1)S(1)}, u32[]{:S(2)}, u32[]{:S(2)}) collective-permute-start(bf16[160,512]{1,0:T(8,128)(2,1)S(1)} %maximum_select_fusion.15), channel_id=1, source_target_pairs={{0,16},{4,20},{8,24},{12,28},{16,0},{20,4},{24,8},{28,12},{1,17},{... | collective-permute-start | bytes 491528 | tf_op jit(solution)/shard_map/ppermute | solution.py:324
  232.5 13.9 %collective-permute-start.51 = (bf16[320,512]{1,0:T(8,128)(2,1)S(1)}, bf16[320,512]{1,0:T(8,128)(2,1)S(1)}, u32[]{:S(2)}, u32[]{:S(2)}) collective-permute-start(bf16[320,512]{1,0:T(8,128)(2,1)S(1)} %maximum_select_fusion.12), channel_id=1, source_target_pairs={{0,2},{1,3},{2,0},{3,1},{4,6},{5,7},{6,4},{7,5},{8,10},{9,11},{10,... | collective-permute-start | bytes 983048 | tf_op jit(solution)/shard_map/ppermute | solution.py:324
  238.3 19.7 %collective-permute-start.18 = (bf16[256,512]{1,0:T(8,128)(2,1)S(1)}, bf16[256,512]{1,0:T(8,128)(2,1)S(1)}, u32[]{:S(2)}, u32[]{:S(2)}) collective-permute-start(bf16[256,512]{1,0:T(8,128)(2,1)S(1)} %constant_dynamic-slice_fusion.13), channel_id=1, source_target_pairs={{0,4},{4,0},{8,12},{12,8},{16,20},{20,16},{24,28},{28,24},{1,5},{5... | collective-permute-start | bytes 786440 | tf_op jit(solution)/shard_map/ppermute | solution.py:324
  238.6 14.5 %collective-permute-start.43 = (bf16[320,512]{1,0:T(8,128)(2,1)S(1)}, bf16[320,512]{1,0:T(8,128)(2,1)S(1)}, u32[]{:S(2)}, u32[]{:S(2)}) collective-permute-start(bf16[320,512]{1,0:T(8,128)(2,1)S(1)} %maximum_select_fusion.11), channel_id=1, source_target_pairs={{0,8},{4,12},{8,0},{12,4},{16,24},{20,28},{24,16},{28,20},{1,9},{5... | collective-permute-start | bytes 983048 | tf_op jit(solution)/shard_map/ppermute | solution.py:324
  246.7 14.5 %collective-permute-start.52 = (bf16[640,512]{1,0:T(8,128)(2,1)S(1)}, bf16[640,512]{1,0:T(8,128)(2,1)S(1)}, u32[]{:S(2)}, u32[]{:S(2)}) collective-permute-start(bf16[640,512]{1,0:T(8,128)(2,1)S(1)} %maximum_select_fusion.6), channel_id=1, source_target_pairs={{0,8},{4,12},{8,0},{12,4},{16,24},{20,28},{24,16},{28,20},{1,9},{5... | collective-permute-start | bytes 1966088 | tf_op jit(solution)/shard_map/ppermute | solution.py:324
  246.8 40.8 %collective-permute-start.25 = (f32[3,512]{1,0:T(4,128)S(1)}, f32[3,512]{1,0:T(4,128)S(1)}, u32[]{:S(2)}, u32[]{:S(2)}) collective-permute-start(f32[3,512]{1,0:T(4,128)S(1)} %fusion.149), channel_id=1, source_target_pairs={{0,2},{1,3},{2,0},{3,1},{4,6},{5,7},{6,4},{7,5},{8,10},{9,11},{10,... | collective-permute-start | bytes 18440 | tf_op jit(solution)/shard_map/ppermute | solution.py:324
  258.0 15.9 %collective-permute-start.19 = (bf16[128,512]{1,0:T(8,128)(2,1)S(1)}, bf16[128,512]{1,0:T(8,128)(2,1)S(1)}, u32[]{:S(2)}, u32[]{:S(2)}) collective-permute-start(bf16[128,512]{1,0:T(8,128)(2,1)S(1)} %constant_dynamic-slice_fusion.12), channel_id=1, source_target_pairs={{0,8},{4,12},{8,0},{12,4},{16,24},{20,28},{24,16},{28,20},{1,9},{5... | collective-permute-start | bytes 393224 | tf_op jit(solution)/shard_map/ppermute | solution.py:324
  273.9 42.4 %collective-permute-start.53 = (bf16[4096,512]{1,0:T(8,128)(2,1)}, bf16[4096,512]{1,0:T(8,128)(2,1)}, u32[]{:S(2)}, u32[]{:S(2)}) collective-permute-start(bf16[4096,512]{1,0:T(8,128)(2,1)} %get-tuple-element.73), channel_id=1, source_target_pairs={{0,1},{1,0},{2,3},{3,2},{4,5},{5,4},{6,7},{7,6},{8,9},{9,8},{10,11... | collective-permute-start | bytes 12582920 | tf_op jit(solution)/shard_map/ppermute | solution.py:324
  274.0 14.9 %collective-permute-start.20 = (bf16[64,512]{1,0:T(8,128)(2,1)S(1)}, bf16[64,512]{1,0:T(8,128)(2,1)S(1)}, u32[]{:S(2)}, u32[]{:S(2)}) collective-permute-start(bf16[64,512]{1,0:T(8,128)(2,1)S(1)} %constant_dynamic-slice_fusion.11), channel_id=1, source_target_pairs={{0,16},{4,20},{8,24},{12,28},{16,0},{20,4},{24,8},{28,12},{1,17},{... | collective-permute-start | bytes 196616 | tf_op jit(solution)/shard_map/ppermute | solution.py:324
  291.1 12.2 %collective-permute-start.13 = (f32[1,512]{1,0:T(1,128)S(1)}, f32[1,512]{1,0:T(1,128)S(1)}, u32[]{:S(2)}, u32[]{:S(2)}) collective-permute-start(f32[1,512]{1,0:T(1,128)S(1)} %add.310), channel_id=1, source_target_pairs={{0,8},{4,12},{8,0},{12,4},{16,24},{20,28},{24,16},{28,20},{1,9},{5... | collective-permute-start | bytes 6152 | tf_op jit(solution)/shard_map/ppermute | solution.py:324
  291.4 13.0 %collective-permute-start.27 = (f32[3,512]{1,0:T(4,128)S(1)}, f32[3,512]{1,0:T(4,128)S(1)}, u32[]{:S(2)}, u32[]{:S(2)}) collective-permute-start(f32[3,512]{1,0:T(4,128)S(1)} %add.330), channel_id=1, source_target_pairs={{0,8},{4,12},{8,0},{12,4},{16,24},{20,28},{24,16},{28,20},{1,9},{5... | collective-permute-start | bytes 18440 | tf_op jit(solution)/shard_map/ppermute | solution.py:324
  (71 other events, 627.5 us)
